TPU v7x, 32 devices: a whole 2x2x4 slice. The times are simulated.
32 devices in a mesh: aln: 4 (over x, core), seq: 8 (over z, y).
Axes of the slice: x: 2, y: 2, z: 4, core: 2. Of those that a mesh axis runs over, the one named last changes fastest.
Arguments:
- embedded_homologs: bfloat16 [256, 128, 768], P(('aln', 'seq')), parts along dimension 0, may hold values from -6 to 6
- homolog_tallies: int32 [4], P('aln'), parts along dimension 0, may hold values from 16 to 64
- horizontal_probe_matrix: bfloat16 [768, 768], replicated
- horizontal_lookup_matrix: bfloat16 [768, 768], replicated
- horizontal_content_matrix: bfloat16 [768, 768], replicated, may hold values from -0.21875 to 0.21875
- vertical_probe_matrix: bfloat16 [768, 768], replicated
- vertical_lookup_matrix: bfloat16 [768, 768], replicated
- vertical_content_matrix: bfloat16 [768, 768], replicated, may hold values from -0.21875 to 0.21875
Outputs:
- row_output: bfloat16 [256, 128, 768], P(('aln', 'seq')), parts along dimension 0
- column_output: bfloat16 [256, 128, 768], P(('aln', 'seq')), parts along dimension 0
There are 4 independent parts, one for each index of `aln`. A program takes and returns all parts, laid end to end along the dimension named above; an argument that names none is the same for every part. Nothing has to cross between parts.
Inputs may be any that keep to these rules, and one draw needn't show every extreme that they name: Sequence slots from homolog_tallies[0] on are padding.
All inputs are finite; a program needn't handle non-finite values.
Results may differ from a plain program's by a relative error of at most 0.024.
Values may be sent and summed in bfloat16 or wider, within the bound.
A program may use at most 128 MiB of HBM per device.

v0:
```python
import jax
import jax.numpy as jnp
from jax import lax
from jax.sharding import PartitionSpec as P

H = 12
DH = 64


def standardize_features(values):
    centre = jnp.mean(values, axis=-1, keepdims=True)
    spread = jnp.mean((values - centre) ** 2, axis=-1, keepdims=True)
    return (values - centre) * lax.rsqrt(spread + 1e-05)


def project(standardized_activations, weight):
    lead = standardized_activations.shape[:-1]
    flat = standardized_activations.reshape(-1, standardized_activations.shape[-1])
    result = jnp.dot(flat, weight, preferred_element_type=jnp.float32).astype(jnp.bfloat16)
    return result.reshape(lead + (H, DH))


def column_attend(query, key_rows, value_rows, live_all):
    scores = jnp.einsum(
        "schd,tchd->chst", query, key_rows, preferred_element_type=jnp.float32
    ) / jnp.sqrt(jnp.float32(DH))
    scores = jnp.where(live_all[None, None, None, :] > 0, scores, jnp.float32(-1e30))
    weights = jax.nn.softmax(scores, axis=-1).astype(jnp.bfloat16)
    result = jnp.einsum("chst,tchd->schd", weights, value_rows, preferred_element_type=jnp.float32)
    result = (result * live_all[:, None, None, None]).astype(jnp.bfloat16)
    return result.reshape(result.shape[0], 1, result.shape[1], H * DH)


def local(
    embedded_homologs,
    homolog_tallies,
    horizontal_probe_matrix,
    horizontal_lookup_matrix,
    horizontal_content_matrix,
    vertical_probe_matrix,
    vertical_lookup_matrix,
    vertical_content_matrix,
):
    homolog_capacity = embedded_homologs.shape[0]
    position_total = embedded_homologs.shape[1]
    embed_dimension = embedded_homologs.shape[2]
    groups = lax.axis_size("seq")
    count = homolog_tallies[0]
    first = lax.axis_index("seq") * homolog_capacity
    livef = (first + jnp.arange(homolog_capacity, dtype=jnp.int32) < count).astype(jnp.float32)
    standardized_activations = standardize_features(embedded_homologs.astype(jnp.float32)).astype(
        jnp.bfloat16
    )
    rq = project(standardized_activations, horizontal_probe_matrix)
    rk = project(standardized_activations, horizontal_lookup_matrix)
    rv = project(standardized_activations, horizontal_content_matrix)
    masked = rq * livef.astype(jnp.bfloat16)[:, None, None, None]
    partial_value = jnp.einsum("sihd,sjhd->hij", masked, rk, preferred_element_type=jnp.float32)
    scale = jnp.sqrt(jnp.float32(DH)) * jnp.sqrt(count.astype(jnp.float32))
    logits = lax.psum(partial_value.astype(jnp.bfloat16), "seq").astype(jnp.float32) / scale
    weights = jax.nn.softmax(logits, axis=-1).astype(jnp.bfloat16)
    horizontal_mixing_result = jnp.einsum(
        "hij,sjhd->sihd", weights, rv, preferred_element_type=jnp.float32
    )
    horizontal_mixing_result = (
        (horizontal_mixing_result * livef[:, None, None, None])
        .astype(jnp.bfloat16)
        .reshape(homolog_capacity, position_total, embed_dimension)
    )
    intermediate_activations = embedded_homologs.astype(
        jnp.float32
    ) + horizontal_mixing_result.astype(jnp.float32)
    normed2 = standardize_features(intermediate_activations).astype(jnp.bfloat16)
    per_group = position_total // groups
    blocks = normed2.reshape(homolog_capacity, groups, per_group, embed_dimension)
    block = lax.all_to_all(blocks, "seq", split_axis=1, concat_axis=0, tiled=True)
    total = block.shape[0]
    live_all = (jnp.arange(total, dtype=jnp.int32) < count).astype(jnp.float32)
    rows = block.reshape(total, block.shape[2], embed_dimension)
    gathered = column_attend(
        project(rows, vertical_probe_matrix),
        project(rows, vertical_lookup_matrix),
        project(rows, vertical_content_matrix),
        live_all,
    )
    returned = lax.all_to_all(gathered, "seq", split_axis=0, concat_axis=1, tiled=True)
    column_out = returned.reshape(homolog_capacity, position_total, embed_dimension)
    return (horizontal_mixing_result, column_out)


def solution(mesh):
    in_specs = (P(("aln", "seq"), None, None), P("aln"), P(), P(), P(), P(), P(), P())
    out_specs = (P(("aln", "seq"), None, None), P(("aln", "seq"), None, None))
    return jax.shard_map(local, mesh=mesh, in_specs=in_specs, out_specs=out_specs, check_vma=False)
```

profile of v0, /device:TPU:0, one launch (start us, length us, event | category | flops | bytes accessed | tf_op | source)
XLA Modules:
  0.0 255.9 jit_solution(1482950340887383687)
XLA Ops:
  7.2 0.0 copy-start
  7.2 0.0 copy-start.2
  7.2 0.0 all-reduce.2.cloned.1.call-start
  7.2 1.8 convert_reduce_fusion
  9.1 0.1 copy-done.2
  9.2 0.6 fusion.5
  9.8 0.4 fusion.6
  10.2 0.0 copy-start.5
  10.2 1.1 copy-done.5
  11.3 0.0 copy-done
  11.3 2.5 convolution_convert_fusion.4
  13.9 2.6 %copy.48 = bf16[1024,768]{0,1:T(8,128)(2,1)} copy(bf16[1024,768]{1,0:T(8,128)(2,1)} %convolution_convert_fusion.4) | data formatting | bytes 3145728 | tf_op jit(solution)/shard_map/convert_element_type | solution.py:19
  16.5 0.0 copy-start.6
  16.5 0.0 copy-start.7
  16.5 3.2 %copy.65 = bf16[96,8,8,128]{3,2,1,0:T(8,128)(2,1)} copy(bf16[96,8,8,128]{3,1,2,0:T(8,128)(2,1)} %bitcast.59) | data formatting | bytes 3145728
  19.7 0.0 copy-done.6
  19.7 0.0 copy-done.7
  19.7 2.5 convolution_convert_fusion.3
  22.2 2.6 %copy.49 = bf16[1024,768]{0,1:T(8,128)(2,1)} copy(bf16[1024,768]{1,0:T(8,128)(2,1)} %convolution_convert_fusion.3) | data formatting | bytes 3145728 | tf_op jit(solution)/shard_map/convert_element_type | solution.py:19
  24.8 3.0 %copy.66 = bf16[96,8,8,128]{3,2,1,0:T(8,128)(2,1)} copy(bf16[96,8,8,128]{3,1,2,0:T(8,128)(2,1)} %bitcast.60) | data formatting | bytes 3145728
  28.5 3.3 %fusion.31 = bf16[12,128,128]{2,1,0:T(8,128)(2,1)} fusion(bf16[8,128,12,64]{1,0,3,2:T(8,128)(2,1)} %bitcast.73, bf16[8,128,12,64]{1,0,3,2:T(8,128)(2,1)} %bitcast.69, bf16[8]{0:T(256)(128)(2,1)S(1)} %get-tuple-element.8), kind=kOutput, calls=%fused_computation.41 | convolution fusion | flops 202309632 | bytes 3538960 | tf_op jit(solution)/shard_map/sihd,sjhd->hij/dot_general | solution.py:58
  31.8 0.0 all-reduce.2.cloned.1.call-update
  31.9 4.3 %convolution_convert_fusion.5 = bf16[1024,768]{1,0:T(8,128)(2,1)} fusion(bf16[1024,768]{1,0:T(8,128)(2,1)} %bitcast.67, bf16[768,768]{1,0:T(8,128)(2,1)} %param.12), kind=kOutput, calls=%fused_computation.33 | convolution fusion | flops 1208745984 | bytes 4325376 | tf_op jit(solution)/shard_map/dot_general | solution.py:19
  36.2 2.6 %copy.47 = bf16[1024,768]{0,1:T(8,128)(2,1)} copy(bf16[1024,768]{1,0:T(8,128)(2,1)} %convolution_convert_fusion.5) | data formatting | bytes 3145728 | tf_op jit(solution)/shard_map/convert_element_type | solution.py:19
  38.7 3.0 %copy.64 = bf16[96,8,8,128]{3,2,1,0:T(8,128)(2,1)} copy(bf16[96,8,8,128]{3,1,2,0:T(8,128)(2,1)} %bitcast.61) | data formatting | bytes 3145728
  41.8 64.3 %all-reduce.2.cloned.1.call-done = bf16[12,128,128]{2,1,0:T(8,128)(2,1)} async-done(((bf16[12,128,128]{2,1,0:T(8,128)(2,1)}), bf16[12,128,128]{2,1,0:T(8,128)(2,1)}) %all-reduce.2.cloned.1.call-update) | async-done | bytes 393232 | tf_op jit(solution)/shard_map/psum | solution.py:60
  106.0 1.5 fusion.42
  107.5 5.6 %fusion.23 = bf16[8,128,12,64]{1,3,0,2:T(8,128)(2,1)} fusion(f32[8]{0:T(128)S(1)} %get-tuple-element.9, bf16[8,128,12,64]{1,0,3,2:T(8,128)(2,1)} %bitcast.74, f32[12,128]{1,0:T(8,128)S(1)} %fusion.42, bf16[12,128,128]{2,1,0:T(8,128)(2,1)} %all-reduce.2.cloned.1.call-done, f32[]{:T(128)S(6)} %mul_sqrt.3), kind=kOutput, calls=%fused_computation.37 | convolution fusion | flops 203884160 | bytes 3545124 | tf_op jit(solution)/shard_map/hij,sjhd->sihd/dot_general | solution.py:62
  113.2 2.7 %copy.51 = bf16[8,128,12,64]{1,3,2,0:T(8,128)(2,1)} copy(bf16[8,128,12,64]{1,3,0,2:T(8,128)(2,1)} %fusion.23) | data formatting | bytes 3145728 | tf_op jit(solution)/shard_map/convert_element_type | solution.py:67
  115.9 2.6 %copy.60 = bf16[8,128,768]{2,1,0:T(8,128)(2,1)} copy(bf16[8,128,768]{1,2,0:T(8,128)(2,1)} %bitcast.62) | data formatting | bytes 3145728
  118.5 0.0 copy-start.3
  118.5 2.0 fusion.17
  120.5 0.0 copy-done.3
  120.5 0.8 multiply_reduce_fusion
  121.3 0.6 multiply_convert_fusion.1
  121.9 1.3 copy.53
  123.2 0.0 copy-start.8
  123.2 3.9 %all-to-all-start = ((bf16[8,8,16,768]{3,2,0,1:T(8,128)(2,1)}), bf16[8,8,16,768]{3,2,0,1:T(8,128)(2,1)S(1)}, u32[]{:S(2)}, u32[]{:S(2)}) async-start(bf16[8,8,16,768]{3,2,0,1:T(8,128)(2,1)} %copy.53), calls=%async_computation | async-start | bytes 3145728 | tf_op jit(solution)/shard_map/all_to_all | solution.py:76
  127.1 35.7 %all-to-all-done = bf16[8,8,16,768]{3,2,0,1:T(8,128)(2,1)S(1)} async-done(((bf16[8,8,16,768]{3,2,0,1:T(8,128)(2,1)}), bf16[8,8,16,768]{3,2,0,1:T(8,128)(2,1)S(1)}, u32[]{:S(2)}, u32[]{:S(2)}) %all-to-all-start) | async-done | bytes 1572896 | tf_op jit(solution)/shard_map/all_to_all | solution.py:76
  162.8 0.0 copy-done.8
  162.8 2.5 convolution_convert_fusion.1
  165.3 0.0 copy-start.9
  165.3 6.0 %reshape.97 = bf16[64,16,12,64]{3,2,1,0:T(8,128)(2,1)} reshape(bf16[1024,768]{1,0:T(8,128)(2,1)} %convolution_convert_fusion.1) | data formatting | bytes 3145728 | tf_op jit(solution)/shard_map/reshape | solution.py:20
  171.3 0.0 copy-done.9
  171.3 2.5 convolution_convert_fusion
  173.8 0.0 copy-start.10
  173.8 6.0 %reshape.98 = bf16[64,16,12,64]{3,2,1,0:T(8,128)(2,1)} reshape(bf16[1024,768]{1,0:T(8,128)(2,1)} %convolution_convert_fusion) | data formatting | bytes 3145728 | tf_op jit(solution)/shard_map/reshape | solution.py:20
  179.8 0.0 copy-done.10
  179.8 2.5 convolution_convert_fusion.2
  182.3 5.9 %reshape.96 = bf16[64,16,12,64]{3,2,1,0:T(8,128)(2,1)} reshape(bf16[1024,768]{1,0:T(8,128)(2,1)} %convolution_convert_fusion.2) | data formatting | bytes 3145728 | tf_op jit(solution)/shard_map/reshape | solution.py:20
  188.3 7.2 %fusion.9 = f32[16,12,64,64]{2,3,1,0:T(8,128)S(1)} fusion(bf16[64,16,12,64]{3,2,1,0:T(8,128)(2,1)} %reshape.98, bf16[64,16,12,64]{3,2,1,0:T(8,128)(2,1)} %reshape.97), kind=kOutput, calls=%fused_computation.16 | convolution fusion | flops 100663296 | bytes 6291456 | tf_op jit(solution)/shard_map/schd,tchd->chst/dot_general | solution.py:24
  195.5 0.0 copy-start.4
  195.5 2.3 fusion.43
  197.8 0.0 copy-done.4
  197.8 4.1 %multiply_convert_fusion = bf16[16,12,64,64]{3,2,1,0:T(8,128)(2,1)} fusion(f32[64]{0:T(128)S(1)} %get-tuple-element.12, f32[16,12,64,64]{2,3,1,0:T(8,128)S(1)} %get-tuple-element.11, f32[16,12,64]{2,1,0:T(8,128)S(1)} %get-tuple-element.10, bf16[64,16,12,64]{3,2,1,0:T(8,128)(2,1)S(1)} %copy-done.4), kind=kOutput, calls=%fused_computation.2 | convolution fusion | flops 103809024 | bytes 6340864 | tf_op jit(solution)/shard_map/chst,tchd->schd/dot_general | solution.py:29
  202.0 4.9 %copy.58 = bf16[64,1,16,768]{3,2,1,0:T(8,128)(2,1)} copy(bf16[64,1,16,768]{0,3,2,1:T(8,128)(2,1)} %bitcast.65) | data formatting | bytes 3145728 | tf_op jit(solution)/shard_map/reshape | solution.py:31
  206.8 40.6 %all_to_all.30 = bf16[64,1,16,768]{3,2,1,0:T(8,128)(2,1)S(1)} all-to-all(bf16[64,1,16,768]{3,2,1,0:T(8,128)(2,1)} %copy.58), channel_id=1, replica_groups=mesh['aln'=4,'seq'=8] {'seq'}, dimensions={0} | all-to-all | bytes 3145728 | tf_op jit(solution)/shard_map/all_to_all | solution.py:86
  247.4 0.0 copy-start.1
  247.4 1.3 copy.59
  248.7 0.4 copy-done.1
  (6 shorter events, 0.0 us)
Async XLA Ops:
  7.2 4.2 %copy-start = (bf16[768,768]{1,0:T(8,128)(2,1)S(1)}, bf16[768,768]{1,0:T(8,128)(2,1)}, u32[]{:S(2)}) copy-start(bf16[768,768]{1,0:T(8,128)(2,1)} %param.10) | copy-start | bytes 3538948
  7.2 2.0 copy-start.2
  7.2 98.9 %all-reduce.2.cloned.1.call-start = ((), (), s32[]{:S(2)}) async-start(), calls=%async_computation.2 | async-start | bytes 786432 | tf_op jit(solution)/shard_map/psum | solution.py:60
  10.2 1.1 copy-start.5
  16.5 3.2 %copy-start.6 = (bf16[8,128,768]{2,1,0:T(8,128)(2,1)S(1)}, bf16[8,128,768]{2,1,0:T(8,128)(2,1)}, u32[]{:S(2)}) copy-start(bf16[8,128,768]{2,1,0:T(8,128)(2,1)} %copy-done.5) | copy-start | bytes 4718596
  16.5 3.2 %copy-start.7 = (bf16[768,768]{1,0:T(8,128)(2,1)S(1)}, bf16[768,768]{1,0:T(8,128)(2,1)}, u32[]{:S(2)}) copy-start(bf16[768,768]{1,0:T(8,128)(2,1)} %param.11) | copy-start | bytes 3538948
  118.5 2.0 copy-start.3
  123.2 39.6 %copy-start.8 = (bf16[768,768]{1,0:T(8,128)(2,1)S(1)}, bf16[768,768]{1,0:T(8,128)(2,1)}, u32[]{:S(2)}) copy-start(bf16[768,768]{1,0:T(8,128)(2,1)} %param.13) | copy-start | bytes 3538948
  123.2 39.6 %all-to-all-start = ((bf16[8,8,16,768]{3,2,0,1:T(8,128)(2,1)}), bf16[8,8,16,768]{3,2,0,1:T(8,128)(2,1)S(1)}, u32[]{:S(2)}, u32[]{:S(2)}) async-start(bf16[8,8,16,768]{3,2,0,1:T(8,128)(2,1)} %copy.53), calls=%async_computation | async-start | bytes 3145728 | tf_op jit(solution)/shard_map/all_to_all | solution.py:76
  165.3 6.0 %copy-start.9 = (bf16[768,768]{1,0:T(8,128)(2,1)S(1)}, bf16[768,768]{1,0:T(8,128)(2,1)}, u32[]{:S(2)}) copy-start(bf16[768,768]{1,0:T(8,128)(2,1)} %param.14) | copy-start | bytes 3538948
  173.8 6.0 %copy-start.10 = (bf16[768,768]{1,0:T(8,128)(2,1)S(1)}, bf16[768,768]{1,0:T(8,128)(2,1)}, u32[]{:S(2)}) copy-start(bf16[768,768]{1,0:T(8,128)(2,1)} %param.15) | copy-start | bytes 3538948
  195.5 2.4 copy-start.4
  247.4 1.7 copy-start.1
Sparse Core Ops, SparseCore 0:
  32.0 74.0 all-reduce.1
where the time goes:
time: 257 us; the launch traced here: 256 us
  waiting for transfers between devices  100 us (39%)
  local copies, waits for them, and re-layouts  49.2 us (19%)
  blocking collectives  40.6 us (16%)
  matrix products  37.3 us (15%)
  between operations  14.9 us (6%)
  other arithmetic  10.1 us (4%)
  starting transfers between devices  3.93 us (2%)
    psum x1, waiting for transfers between devices, local(): lax.psum(partial_value.astype(jnp.bfloat16), 'seq').astype(jnp.float32)  64.3 us
    all_to_all x1, blocking collectives, local(): lax.all_to_all(gathered, 'seq', split_axis=0, concat_axis=1, tiled=True)  40.6 us
    all_to_all x1, waiting for transfers between devices, local(): lax.all_to_all(blocks, 'seq', split_axis=1, concat_axis=0, tiled=True)  35.7 us
    reshape x3, local copies, waits for them, and re-layouts, project(): return result.reshape(lead + (H, DH))  17.9 us
    dot_general x6, matrix products, project(): jnp.dot(flat, weight, preferred_element_type=jnp.float32)  17 us
    unnamed x26, local copies, waits for them, and re-layouts  13.5 us
    convert_element_type x3, local copies, waits for them, and re-layouts, project(): jnp.dot(flat, weight, preferred_element_type=jnp.float32)  7.76 us
    dot_general x1, matrix products, column_attend(): jnp.einsum('schd,tchd->chst', query, key_rows, preferred_element_type=jnp...  7.2 us
  transfers between devices with their start and end apart: 2, of which 2 were waited for; matrix products, arithmetic and copies ran while one was open for 4% of the time, Pallas kernels for 0%

commit v1 on v0

v1 whole, which is shorter than its diff:
```python
import functools

import jax
import jax.numpy as jnp
import numpy as np
from jax import lax
from jax.experimental import pallas as pl
from jax.experimental.pallas import tpu as pltpu
from jax.sharding import PartitionSpec as P

DH = 64
PAIR = 2 * DH
GROUP = 2 * PAIR
F32 = jnp.float32
BF16 = jnp.bfloat16
MESH = pl.DeviceIdType.MESH


def standardize(values):
    centre = jnp.mean(values, axis=-1, keepdims=True)
    shifted = values - centre
    spread = jnp.mean(shifted * shifted, axis=-1, keepdims=True)
    return shifted * lax.rsqrt(spread + 1e-05)


def softmax(scores):
    e = jnp.exp(scores - jnp.max(scores, axis=-1, keepdims=True))
    return (e * (1.0 / jnp.sum(e, axis=-1, keepdims=True))).astype(BF16)


def dot(a, b):
    return jnp.dot(a, b, preferred_element_type=F32)


def dot_t(a, b):
    return lax.dot_general(a, b, (((1,), (1,)), ((), ())), preferred_element_type=F32)


def kernel(
    n, seqs, length, width,
    count_ref, inv_ref, x_hbm, hq_hbm, hk_hbm, hv_hbm, vq_hbm, vk_hbm, vv_hbm, there_hbm, back_hbm,
    row_hbm, col_hbm,
    x, hq, hk, hv, vq, vk, vv, there, back,
    normed, rq, rk, rv, part, part_in, weights, row_out, send, arrived, cq, ck, cv, ret, ret_in, out,
    load_sem, rs_s, rs_r, ag_s, ag_r, go_s, go_r, re_s, re_r,
):
    per = length // n
    rows = seqs * length
    block = seqs * per
    pair_rows = 2 * seqs
    pairs = per // 2
    step_pairs = min(2, pairs)
    steps = pairs // step_pairs
    step_rows = step_pairs * pair_rows
    span = n * pair_rows
    groups = width // GROUP
    group_rows = (GROUP // DH) * length
    share = group_rows // n
    me = lax.axis_index("seq")
    count = count_ref[0]
    inverse = inv_ref[0]

    loads = [
        pltpu.make_async_copy(src, dst, load_sem.at[at])
        for at, (src, dst) in enumerate(
            [(x_hbm, x), (hq_hbm, hq), (hk_hbm, hk), (hv_hbm, hv), (there_hbm, there),
             (vq_hbm, vq), (vk_hbm, vk), (vv_hbm, vv), (back_hbm, back)]
        )
    ]
    for load in loads:
        load.start()

    barrier = pltpu.get_barrier_semaphore()

    def greet(k, c):
        pl.semaphore_signal(
            barrier, inc=1, device_id={"seq": lax.rem(me + k, n)}, device_id_type=MESH
        )
        return c

    lax.fori_loop(1, n, greet, 0)

    def target(k):
        return lax.rem(me + k, n)

    def source(k):
        return lax.rem(me + n - k, n)

    def aligned(index, size):
        return pl.ds(pl.multiple_of(index * size, size), size)

    def remote(src, dst, s, r, to):
        return pltpu.make_async_remote_copy(
            src_ref=src, dst_ref=dst, send_sem=s, recv_sem=r, device_id={"seq": to},
            device_id_type=MESH,
        )

    def rs_copy(g, k):
        return remote(
            part.at[g, aligned(target(k), share)], part_in.at[g, k], rs_s.at[g, k], rs_r.at[g, k],
            target(k),
        )

    def ag_copy(g, k, owner):
        at = aligned(owner, share)
        return remote(
            weights.at[g, at], weights.at[g, at], ag_s.at[g, k], ag_r.at[g, k], target(k)
        )

    def go_copy(t, k, owner):
        at = aligned(t, step_rows)
        return remote(
            send.at[target(k), at], arrived.at[owner, at], go_s.at[t, k], go_r.at[t, k], target(k)
        )

    def re_copy(t, k, owner):
        at = aligned(t, step_rows)
        return remote(
            ret.at[target(k), at], ret_in.at[owner, at], re_s.at[t, k], re_r.at[t, k], target(k)
        )

    lane = lax.broadcasted_iota(jnp.int32, (1, PAIR), 1)
    left = jnp.where(lane < DH, 1.0, 0.0).astype(BF16)
    right = jnp.where(lane < DH, 0.0, 1.0).astype(BF16)

    loads[0].wait()

    def norm_one(s, c):
        at = aligned(s, length)
        normed[at] = standardize(x[s].astype(F32)).astype(BF16)
        return c

    lax.fori_loop(0, seqs, norm_one, 0)
    loads[1].wait()
    loads[2].wait()

    def side(ref, lanes):
        return jnp.concatenate(
            [ref[s * length:(s + 1) * length, lanes] for s in range(seqs)], axis=1
        )

    tile = 2 * length
    for g in range(groups):
        lanes = slice(g * GROUP, (g + 1) * GROUP)

        def project(r, c, lanes=lanes):
            at = aligned(r, tile)
            a = normed[at]
            slot = lax.broadcasted_iota(jnp.int32, (tile, 1), 0)
            first = me * seqs + r * 2
            live = jnp.where(
                jnp.where(slot < length, first, first + 1) < count, 1.0, 0.0
            ).astype(F32)
            rq[at, lanes] = (dot(a, hq[:, lanes]) * live).astype(BF16)
            rk[at, lanes] = dot(a, hk[:, lanes]).astype(BF16)
            return c

        lax.fori_loop(0, rows // tile, project, 0)
        left_s = jnp.concatenate([left] * seqs, axis=1)
        right_s = jnp.concatenate([right] * seqs, axis=1)
        for p in range(GROUP // PAIR):
            pl_lanes = slice(g * GROUP + p * PAIR, g * GROUP + (p + 1) * PAIR)
            q = side(rq, pl_lanes)
            q2 = jnp.concatenate([q * left_s, q * right_s], axis=0)
            part[g, p * 2 * length:(p + 1) * 2 * length, :] = dot_t(q2, side(rk, pl_lanes)).astype(BF16)
        if g == 0:
            pl.semaphore_wait(barrier, n - 1)

        def rs_start(k, c, g=g):
            rs_copy(g, k).start()
            return c

        lax.fori_loop(1, n, rs_start, 0)

    loads[3].wait()

    def project_v(r, c):
        at = aligned(r, tile)
        rv[at] = dot(normed[at], hv[...]).astype(BF16)
        return c

    lax.fori_loop(0, rows // tile, project_v, 0)

    for g in range(groups):
        def add(k, total, g=g):
            rs_copy(g, k).wait_recv()
            return total + part_in[g, k].astype(F32)

        logits = lax.fori_loop(1, n, add, part[g, aligned(me, share), :].astype(F32))
        weights[g, aligned(me, share), :] = softmax(logits * inverse)

        def ag_start(k, c, g=g):
            ag_copy(g, k, me).start()
            return c

        lax.fori_loop(1, n, ag_start, 0)

    for g in range(groups):
        def ag_wait(k, c, g=g):
            ag_copy(g, k, source(k)).wait_recv()
            return c

        lax.fori_loop(1, n, ag_wait, 0)
        left_s = jnp.concatenate([left] * seqs, axis=1)
        right_s = jnp.concatenate([right] * seqs, axis=1)
        for p in range(GROUP // PAIR):
            lanes = slice(g * GROUP + p * PAIR, g * GROUP + (p + 1) * PAIR)
            w2 = jnp.concatenate(
                [weights[g, (2 * p + i) * length:(2 * p + i + 1) * length, :] for i in range(2)],
                axis=1,
            )
            v = side(rv, lanes)
            mixed = dot(w2, jnp.concatenate([v * left_s, v * right_s], axis=0))
            for s in range(seqs):
                live = jnp.where(me * seqs + s < count, 1.0, 0.0).astype(F32)
                row_out[s, :, lanes] = (mixed[:, s * PAIR:(s + 1) * PAIR] * live).astype(BF16)

    row_copy = pltpu.make_async_copy(row_out, row_hbm, load_sem.at[len(loads)])
    row_copy.start()

    loads[4].wait()
    if per % 16 == 0:
        for d in range(n):
            at = slice(d * per, (d + 1) * per)
            a = x[:, at, :].astype(F32) + row_out[:, at, :].astype(F32)
            a = standardize(a).astype(BF16).reshape(block, width)
            send[d] = dot(there[...], a).astype(BF16)
    else:
        def norm_two(s, c):
            normed[aligned(s, length)] = standardize(
                x[s].astype(F32) + row_out[s].astype(F32)
            ).astype(BF16)
            return c

        lax.fori_loop(0, seqs, norm_two, 0)
        for d in range(n):
            send[d] = dot(there[d * block:(d + 1) * block, :], normed[...]).astype(BF16)

    def go_step(t, c):
        def go_start(k, c):
            go_copy(t, k, me).start()
            return c

        return lax.fori_loop(1, n, go_start, c)

    lax.fori_loop(0, steps, go_step, 0)
    arrived[me] = send[me]
    for load in loads[5:]:
        load.wait()

    shift = seqs.bit_length() - 1
    shape = (2 * span, span)

    def place(index):
        return lax.shift_left(lax.shift_right_logical(index, shift + 1), shift) + (index & (seqs - 1))

    def column(index):
        return lax.shift_right_logical(index, shift) & 1

    key = lax.broadcasted_iota(jnp.int32, shape, 1)
    query = lax.broadcasted_iota(jnp.int32, shape, 0)
    open_f = jnp.where(
        (column(key) == column(query)) & (place(key) < count), 1.0, 0.0
    )
    live_q = jnp.where(
        place(lax.broadcasted_iota(jnp.int32, (span, 1), 0)) < count, 1.0, 0.0
    ).astype(F32)

    def attend_step(t, c):
        def go_wait(k, c):
            go_copy(t, k, source(k)).wait_recv()
            return c

        lax.fori_loop(1, n, go_wait, 0)
        a = jnp.concatenate(
            [
                arrived[:, pl.ds(pl.multiple_of(t * step_rows + p * pair_rows, pair_rows), pair_rows), :]
                .reshape(span, width)
                for p in range(step_pairs)
            ],
            axis=0,
        )
        cq[...] = (dot(a, vq[...]) * (DH ** -0.5)).astype(BF16)
        ck[...] = dot(a, vk[...]).astype(BF16)
        cv[...] = dot(a, vv[...]).astype(BF16)

        def attend_pair(p, c):
            at = aligned(p, span)
            out_at = pl.ds(
                pl.multiple_of(t * step_rows + p * pair_rows, pair_rows), pair_rows
            )
            for h in range(width // PAIR):
                lanes = slice(h * PAIR, (h + 1) * PAIR)
                q = cq[at, lanes]
                scores = dot_t(jnp.concatenate([q * left, q * right], axis=0), ck[at, lanes])
                w = softmax(jnp.where(open_f > 0.5, scores, -1e30))
                w2 = jnp.concatenate([w[:span], w[span:]], axis=1)
                v = cv[at, lanes]
                o = dot(w2, jnp.concatenate([v * left, v * right], axis=0))
                ret[:, out_at, lanes] = (o * live_q).astype(BF16).reshape(n, pair_rows, PAIR)
            return c

        lax.fori_loop(0, step_pairs, attend_pair, 0)

        def re_start(k, c):
            re_copy(t, k, me).start()
            return c

        return lax.fori_loop(1, n, re_start, c)

    lax.fori_loop(0, steps, attend_step, 0)
    ret_in[me] = ret[me]

    def re_wait(t, c):
        def one(k, c):
            re_copy(t, k, source(k)).wait_recv()
            return c

        return lax.fori_loop(1, n, one, c)

    lax.fori_loop(0, steps, re_wait, 0)
    if per % 16 == 0:
        for d in range(n):
            out[:, d * per:(d + 1) * per, :] = (
                dot(back[...], ret_in[d]).astype(BF16).reshape(seqs, per, width)
            )
    else:
        flat = ret_in[...].reshape(n * block, width)
        for s in range(seqs):
            out[s] = dot(back[s * length:(s + 1) * length, :], flat).astype(BF16)
    col_copy = pltpu.make_async_copy(out, col_hbm, load_sem.at[len(loads) + 1])
    col_copy.start()

    def sent(k, c):
        for g in range(groups):
            rs_copy(g, k).wait_send()
            ag_copy(g, k, me).wait_send()
        for t in range(steps):
            go_copy(t, k, me).wait_send()
            re_copy(t, k, me).wait_send()
        return c

    lax.fori_loop(1, n, sent, 0)
    row_copy.wait()
    col_copy.wait()


def local(x, tallies, hq, hk, hv, vq, vk, vv):
    seqs, length, width = x.shape
    n = lax.axis_size("seq")
    per = length // n
    block = seqs * per
    groups = width // GROUP
    share = (GROUP // DH) * length // n
    pairs = per // 2
    step_pairs = min(2, pairs)
    steps = pairs // step_pairs
    span = n * 2 * seqs
    if per % 16 == 0:
        order = np.arange(block).reshape(seqs, per).T.reshape(-1)
    else:
        order = np.arange(n * block).reshape(seqs, n, per).transpose(1, 2, 0).reshape(-1)
    there = np.zeros((order.size, order.size), np.float32)
    there[np.arange(order.size), order] = 1.0
    inverse = 1.0 / (jnp.sqrt(F32(DH)) * jnp.sqrt(tallies.astype(F32)))
    any_spec = pl.BlockSpec(memory_space=pl.ANY)
    smem_spec = pl.BlockSpec(memory_space=pltpu.SMEM)
    rows = seqs * length

    def vmem(*shape):
        return pltpu.VMEM(shape, BF16)

    def dma(*shape):
        return pltpu.SemaphoreType.DMA(shape)

    return pl.pallas_call(
        functools.partial(kernel, n, seqs, length, width),
        out_shape=(jax.ShapeDtypeStruct(x.shape, BF16), jax.ShapeDtypeStruct(x.shape, BF16)),
        in_specs=[smem_spec, smem_spec] + [any_spec] * 9,
        out_specs=(any_spec, any_spec),
        scratch_shapes=[
            vmem(*x.shape),
            *[vmem(width, width) for _ in range(6)],
            vmem(order.size, order.size),
            vmem(order.size, order.size),
            vmem(rows, width),
            vmem(rows, width),
            vmem(rows, width),
            vmem(rows, width),
            vmem(groups, n * share, length),
            vmem(groups, n, share, length),
            vmem(groups, n * share, length),
            vmem(*x.shape),
            vmem(n, block, width),
            vmem(n, block, width),
            vmem(step_pairs * span, width),
            vmem(step_pairs * span, width),
            vmem(step_pairs * span, width),
            vmem(n, block, width),
            vmem(n, block, width),
            vmem(*x.shape),
            dma(11),
            dma(groups, n), dma(groups, n), dma(groups, n), dma(groups, n),
            dma(steps, n), dma(steps, n), dma(steps, n), dma(steps, n),
        ],
        compiler_params=pltpu.CompilerParams(
            collective_id=0, has_side_effects=True, vmem_limit_bytes=56 * 1024 * 1024
        ),
    )(tallies, inverse, x, hq, hk, hv, vq, vk, vv, jnp.asarray(there, BF16), jnp.asarray(there.T, BF16))


def solution(mesh):
    in_specs = (P(("aln", "seq"), None, None), P("aln"), P(), P(), P(), P(), P(), P())
    out_specs = (P(("aln", "seq"), None, None), P(("aln", "seq"), None, None))
    return jax.shard_map(local, mesh=mesh, in_specs=in_specs, out_specs=out_specs, check_vma=False)
```

time: 257 us -> 105 us (0.41)
  waiting for transfers between devices: 100 us -> 0 us
  Pallas kernels: 0 us -> 99.1 us
  local copies, waits for them, and re-layouts: 49.2 us -> 3.92 us
  blocking collectives: 40.6 us -> 0 us
  matrix products: 37.3 us -> 0 us
  between operations: 14.9 us -> 1.38 us
  other arithmetic: 10.1 us -> 0 us
  starting transfers between devices: 3.93 us -> 0 us
    pallas_call x0 -> x1, Pallas kernels: none -> 99.1 us  [local(): pl.pallas_call(functools.partial(kernel, n, seqs, length, width), out_sha...]
    psum x1 -> x0, waiting for transfers between devices: 64.3 us -> none  [local(): lax.psum(partial_value.astype(jnp.bfloat16), 'seq').astype(jnp.float32)]
    all_to_all x1 -> x0, blocking collectives: 40.6 us -> none  [local(): lax.all_to_all(gathered, 'seq', split_axis=0, concat_axis=1, tiled=True)]
    dot_general x10 -> x0, matrix products: 37.3 us -> none  [the longest x6 17 us: project(): jnp.dot(flat, weight, preferred_element_type=jnp.float32)]
    all_to_all x1 -> x0, waiting for transfers between devices: 35.7 us -> none  [local(): lax.all_to_all(blocks, 'seq', split_axis=1, concat_axis=0, tiled=True)]
    reshape x5 -> x0, local copies, waits for them, and re-layouts: 24 us -> none  [the longest x3 17.9 us: project(): return result.reshape(lead + (H, DH))]
    convert_element_type x4 -> x0, local copies, waits for them, and re-layouts: 10.5 us -> none  [the longest x3 7.76 us: project(): jnp.dot(flat, weight, preferred_element_type=jnp.float32)]
    unnamed x26 -> x4, local copies, waits for them, and re-layouts: 13.5 us -> 3.92 us
  transfers between devices with their start and end apart: 2 -> 0, of which waited for: 2 -> 0; matrix products, arithmetic and copies ran while one was open for 4% -> 0% of each run, Pallas kernels for 0% -> 0%
where the time goes in v1:
time: 105 us; the launch traced here: 104 us
  Pallas kernels  99.1 us (94%)
  local copies, waits for them, and re-layouts  3.92 us (4%)
  between operations  1.38 us (1%)
    pallas_call x1, Pallas kernels, local(): pl.pallas_call(functools.partial(kernel, n, seqs, length, width), out_sha...  99.1 us
    unnamed x4, local copies, waits for them, and re-layouts  3.92 us

profile of v1, /device:TPU:0, one launch (start us, length us, event | category | flops | bytes accessed | tf_op | source)
XLA Modules:
  0.0 104.4 jit_solution(17102688421838418342)
XLA Ops:
  1.4 99.1 %shard_map.113 = (bf16[8,128,768]{2,1,0:T(8,128)(2,1)}, bf16[8,128,768]{2,1,0:T(8,128)(2,1)}) custom-call(s32[1]{0:T(128)S(6)} %copy.14.count_ref, f32[1]{0:T(128)S(6)} %div.3.inv_ref, bf16[8,128,768]{2,1,0:T(8,128)(2,1)} %x_hbm.1, bf16[768,768]{1,0:T(8,128)(2,1)} %hq_hbm.1, bf16[768,768]{1,0:T(8,128)(2,1)} %hk_hbm.1, bf16[768,768]{1,0:T(8,128)(2,1)} %hv_hbm.1, ...), custom_call_target="tpu_custom_call" | custom-call | tf_op jit(solution)/shard_map/pallas_call | solution.py:376
  100.4 0.0 copy-start
  100.5 2.8 %copy.15 = bf16[8,128,768]{2,1,0:T(8,128)(2,1)} copy(bf16[8,128,768]{2,1,0:T(8,128)(2,1)} %get-tuple-element.4) | data formatting | bytes 3145728
  103.2 0.0 copy-done
  103.2 1.1 %copy.16 = bf16[8,128,768]{2,1,0:T(8,128)(2,1)} copy(bf16[8,128,768]{2,1,0:T(8,128)(2,1)S(1)} %copy-done) | data formatting | bytes 3145728
Async XLA Ops:
  100.4 2.8 %copy-start = (bf16[8,128,768]{2,1,0:T(8,128)(2,1)S(1)}, bf16[8,128,768]{2,1,0:T(8,128)(2,1)}, u32[]{:S(2)}) copy-start(bf16[8,128,768]{2,1,0:T(8,128)(2,1)} %get-tuple-element.5) | copy-start | bytes 4718596

commit v2 on v1

v2 whole, which is shorter than its diff:
```python
import functools

import jax
import jax.numpy as jnp
import numpy as np
from jax import lax
from jax.experimental import pallas as pl
from jax.experimental.pallas import tpu as pltpu
from jax.sharding import PartitionSpec as P

DH = 64
PAIR = 2 * DH
GROUP = 2 * PAIR
STEP_PAIRS = 2
F32 = jnp.float32
BF16 = jnp.bfloat16
MESH = pl.DeviceIdType.MESH


def standardize(values):
    centre = jnp.mean(values, axis=-1, keepdims=True)
    shifted = values - centre
    spread = jnp.mean(shifted * shifted, axis=-1, keepdims=True)
    return shifted * lax.rsqrt(spread + 1e-05)


def softmax(scores):
    e = jnp.exp(scores - jnp.max(scores, axis=-1, keepdims=True))
    return (e * (1.0 / jnp.sum(e, axis=-1, keepdims=True))).astype(BF16)


def dot(a, b):
    return jnp.dot(a, b, preferred_element_type=F32)


def dot_t(a, b):
    return lax.dot_general(a, b, (((1,), (1,)), ((), ())), preferred_element_type=F32)


def kernel(
    n, seqs, length, width,
    count_ref, inv_ref, x_hbm, hq_hbm, hk_hbm, hv_hbm, vq_hbm, vk_hbm, vv_hbm, there_hbm, back_hbm,
    row_hbm, col_hbm,
    x, hq, hk, hv, vq, vk, vv, there, back,
    normed, rq, rk, rv, part, part_in, half_sum, half_in, weights, row_out,
    send, arrived, cq, ck, cv, ret, ret_in, out,
    load_sem, rs_s, rs_r, ex_s, ex_r, ag_s, ag_r, go_s, go_r, re_s, re_r,
):
    half = n // 2
    per = length // n
    rows = seqs * length
    pair_rows = 2 * seqs
    step_pairs = min(STEP_PAIRS, per // 2)
    steps = per // 2 // step_pairs
    step_rows = step_pairs * pair_rows
    step_columns = n * step_pairs * 2
    span = n * pair_rows
    groups = width // GROUP
    share = (GROUP // DH) * length // half
    me = lax.axis_index("seq")
    side_of_me = me // half
    place_of_me = lax.rem(me, half)
    count = count_ref[0]
    inverse = inv_ref[0]

    loads = [
        pltpu.make_async_copy(src, dst, load_sem.at[at])
        for at, (src, dst) in enumerate(
            [(x_hbm, x), (hq_hbm, hq), (hk_hbm, hk), (hv_hbm, hv), (there_hbm, there),
             (vq_hbm, vq), (vk_hbm, vk), (vv_hbm, vv), (back_hbm, back)]
        )
    ]
    for load in loads:
        load.start()

    barrier = pltpu.get_barrier_semaphore()

    def greet(k, c):
        pl.semaphore_signal(
            barrier, inc=1, device_id={"seq": lax.rem(me + k, n)}, device_id_type=MESH
        )
        return c

    lax.fori_loop(1, n, greet, 0)

    def target(k):
        side = lax.rem(side_of_me + 1 + k // half, 2)
        return side * half + lax.rem(place_of_me + k, half)

    def source(k):
        side = lax.rem(side_of_me + 1 + k // half, 2)
        return side * half + lax.rem(place_of_me + n - k, half)

    def aligned(index, size):
        return pl.ds(pl.multiple_of(index * size, size), size)

    def remote(src, dst, s, r, to):
        return pltpu.make_async_remote_copy(
            src_ref=src, dst_ref=dst, send_sem=s, recv_sem=r, device_id={"seq": to},
            device_id_type=MESH,
        )

    def each(body):
        def one(k, c):
            body(k)
            return c

        lax.fori_loop(0, half, one, 0)
        lax.fori_loop(half + 1, n, one, 0)

    def near(body):
        def one(j, c):
            body(j)
            return c

        lax.fori_loop(1, half, one, 0)

    def rs_copy(g, j):
        at = aligned(lax.rem(place_of_me + j, half), share)
        return remote(
            part.at[g, at], part_in.at[g, j], rs_s.at[g, j], rs_r.at[g, j], target(half + j)
        )

    def ex_copy(g):
        return remote(half_sum.at[g], half_in.at[g], ex_s.at[g], ex_r.at[g], target(0))

    def ag_copy(g, j, owner):
        at = aligned(lax.rem(owner, half), share)
        return remote(
            weights.at[g, at], weights.at[g, at], ag_s.at[g, j], ag_r.at[g, j], target(half + j)
        )

    def go_copy(t, k, owner):
        return remote(
            send.at[t, aligned(target(k), step_rows)], arrived.at[t, aligned(owner, step_rows)],
            go_s.at[t, k], go_r.at[t, k], target(k),
        )

    def re_copy(t, k, owner):
        return remote(
            ret.at[t, target(k)], ret_in.at[t, aligned(owner, step_rows)],
            re_s.at[t, k], re_r.at[t, k], target(k),
        )

    lane = lax.broadcasted_iota(jnp.int32, (1, PAIR), 1)
    left = jnp.where(lane < DH, 1.0, 0.0).astype(BF16)
    right = jnp.where(lane < DH, 0.0, 1.0).astype(BF16)
    left_s = jnp.concatenate([left] * seqs, axis=1)
    right_s = jnp.concatenate([right] * seqs, axis=1)

    loads[0].wait()

    def norm_one(s, c):
        normed[aligned(s, length)] = standardize(x[s].astype(F32)).astype(BF16)
        return c

    lax.fori_loop(0, seqs, norm_one, 0)
    loads[1].wait()
    loads[2].wait()

    def beside(ref, lanes):
        return jnp.concatenate(
            [ref[s * length:(s + 1) * length, lanes] for s in range(seqs)], axis=1
        )

    tile = 2 * length

    def project_v(r, c):
        at = aligned(r, tile)
        rv[at] = dot(normed[at], hv[...]).astype(BF16)
        return c

    def logits_of(g):
        lanes = slice(g * GROUP, (g + 1) * GROUP)

        def project(r, c):
            at = aligned(r, tile)
            a = normed[at]
            slot = lax.broadcasted_iota(jnp.int32, (tile, 1), 0)
            first = me * seqs + r * 2
            live = jnp.where(
                jnp.where(slot < length, first, first + 1) < count, 1.0, 0.0
            ).astype(F32)
            rq[at, lanes] = (dot(a, hq[:, lanes]) * live).astype(BF16)
            rk[at, lanes] = dot(a, hk[:, lanes]).astype(BF16)
            return c

        lax.fori_loop(0, rows // tile, project, 0)
        for p in range(GROUP // PAIR):
            two = slice(g * GROUP + p * PAIR, g * GROUP + (p + 1) * PAIR)
            q = beside(rq, two)
            q2 = jnp.concatenate([q * left_s, q * right_s], axis=0)
            part[g, p * tile:(p + 1) * tile, :] = dot_t(q2, beside(rk, two)).astype(BF16)
        if g == 0:
            pl.semaphore_wait(barrier, n - 1)
        near(lambda j: rs_copy(g, j).start())

    def exchange(g):
        def add(j, total):
            rs_copy(g, j).wait_recv()
            return total + part_in[g, j].astype(F32)

        mine = part[g, aligned(place_of_me, share), :].astype(F32)
        half_sum[g] = lax.fori_loop(1, half, add, mine).astype(BF16)
        ex_copy(g).start()

    def weigh(g):
        ex_copy(g).wait_recv()
        logits = half_sum[g].astype(F32) + half_in[g].astype(F32)
        weights[g, aligned(place_of_me, share), :] = softmax(logits * inverse)
        near(lambda j: ag_copy(g, j, me).start())

    for g in range(groups):
        logits_of(g)
        if g > 0:
            exchange(g - 1)
    loads[3].wait()
    lax.fori_loop(0, rows // tile // 2, project_v, 0)
    exchange(groups - 1)
    weigh(0)
    lax.fori_loop(rows // tile // 2, rows // tile, project_v, 0)
    for g in range(1, groups):
        weigh(g)

    for g in range(groups):
        near(lambda j: ag_copy(g, j, source(half + j)).wait_recv())
        for p in range(GROUP // PAIR):
            lanes = slice(g * GROUP + p * PAIR, g * GROUP + (p + 1) * PAIR)
            w2 = jnp.concatenate(
                [weights[g, (2 * p + i) * length:(2 * p + i + 1) * length, :] for i in range(2)],
                axis=1,
            )
            v = beside(rv, lanes)
            mixed = dot(w2, jnp.concatenate([v * left_s, v * right_s], axis=0))
            for s in range(seqs):
                live = jnp.where(me * seqs + s < count, 1.0, 0.0).astype(F32)
                row_out[s, :, lanes] = (mixed[:, s * PAIR:(s + 1) * PAIR] * live).astype(BF16)

    row_copy = pltpu.make_async_copy(row_out, row_hbm, load_sem.at[len(loads)])
    row_copy.start()

    loads[4].wait()

    def go_step(t, c):
        at = aligned(t, step_columns)
        a = x[:, at, :].astype(F32) + row_out[:, at, :].astype(F32)
        a = standardize(a).astype(BF16).reshape(seqs * step_columns, width)
        send[t] = dot(there[...], a).astype(BF16)
        each(lambda k: go_copy(t, k, me).start())
        own = aligned(me, step_rows)
        arrived[t, own, :] = send[t, own, :]
        return c

    lax.fori_loop(0, steps, go_step, 0)
    for load in loads[5:]:
        load.wait()

    shift = seqs.bit_length() - 1
    shape = (2 * span, span)

    def place(index):
        return lax.shift_left(lax.shift_right_logical(index, shift + 1), shift) + (index & (seqs - 1))

    def column(index):
        return lax.shift_right_logical(index, shift) & 1

    key = lax.broadcasted_iota(jnp.int32, shape, 1)
    query = lax.broadcasted_iota(jnp.int32, shape, 0)
    open_f = jnp.where(
        (column(key) == column(query)) & (place(key) < count), 1.0, 0.0
    )
    live_q = jnp.where(
        place(lax.broadcasted_iota(jnp.int32, (span, 1), 0)) < count, 1.0, 0.0
    ).astype(F32)

    def attend_step(t, c):
        each(lambda k: go_copy(t, k, source(k)).wait_recv())
        a = arrived[t].reshape(n, step_rows, width)
        a = jnp.concatenate(
            [
                a[:, p * pair_rows:(p + 1) * pair_rows, :].reshape(span, width)
                for p in range(step_pairs)
            ],
            axis=0,
        )
        cq[...] = (dot(a, vq[...]) * (DH ** -0.5)).astype(BF16)
        ck[...] = dot(a, vk[...]).astype(BF16)
        cv[...] = dot(a, vv[...]).astype(BF16)

        def attend_pair(p, c):
            at = aligned(p, span)
            out_at = aligned(p, pair_rows)
            for h in range(width // PAIR):
                lanes = slice(h * PAIR, (h + 1) * PAIR)
                q = cq[at, lanes]
                scores = dot_t(jnp.concatenate([q * left, q * right], axis=0), ck[at, lanes])
                w = softmax(jnp.where(open_f > 0.5, scores, -1e30))
                w2 = jnp.concatenate([w[:span], w[span:]], axis=1)
                v = cv[at, lanes]
                o = dot(w2, jnp.concatenate([v * left, v * right], axis=0))
                ret[t, :, out_at, lanes] = (o * live_q).astype(BF16).reshape(n, pair_rows, PAIR)
            return c

        lax.fori_loop(0, step_pairs, attend_pair, 0)
        each(lambda k: re_copy(t, k, me).start())
        ret_in[t, aligned(me, step_rows), :] = ret[t, me]
        return c

    lax.fori_loop(0, steps, attend_step, 0)

    def col_copy(t):
        at = aligned(t, step_columns)
        return pltpu.make_async_copy(
            out.at[:, at, :], col_hbm.at[:, at, :], load_sem.at[len(loads) + 1 + t]
        )

    def finish(t, c):
        each(lambda k: re_copy(t, k, source(k)).wait_recv())
        out[:, aligned(t, step_columns), :] = (
            dot(back[...], ret_in[t]).astype(BF16).reshape(seqs, step_columns, width)
        )
        col_copy(t).start()
        return c

    lax.fori_loop(0, steps, finish, 0)

    for g in range(groups):
        near(lambda j: rs_copy(g, j).wait_send())
        ex_copy(g).wait_send()
        near(lambda j: ag_copy(g, j, me).wait_send())

    def sent(t, c):
        each(lambda k: go_copy(t, k, me).wait_send())
        each(lambda k: re_copy(t, k, me).wait_send())
        col_copy(t).wait()
        return c

    lax.fori_loop(0, steps, sent, 0)
    row_copy.wait()


def hand_on(*refs):
    sources, results = refs[:2], refs[2:4]
    held, in_sem, out_sem = refs[4:]
    pieces = [(a, s) for a in range(2) for s in range(sources[0].shape[0])]

    def inward(a, s):
        return pltpu.make_async_copy(sources[a].at[s], held.at[a, s], in_sem.at[a, s])

    def outward(a, s):
        return pltpu.make_async_copy(held.at[a, s], results[a].at[s], out_sem.at[a, s])

    for piece in pieces:
        inward(*piece).start()
    for piece in pieces:
        inward(*piece).wait()
        outward(*piece).start()
    for piece in pieces:
        outward(*piece).wait()


def local(x, tallies, hq, hk, hv, vq, vk, vv):
    seqs, length, width = x.shape
    n = lax.axis_size("seq")
    per = length // n
    groups = width // GROUP
    share = (GROUP // DH) * length // (n // 2)
    step_pairs = min(STEP_PAIRS, per // 2)
    steps = per // 2 // step_pairs
    step_rows = step_pairs * 2 * seqs
    span = n * 2 * seqs
    size = n * step_rows
    order = np.arange(size).reshape(seqs, size // seqs).T.reshape(-1)
    there = np.zeros((size, size), np.float32)
    there[np.arange(size), order] = 1.0
    inverse = 1.0 / (jnp.sqrt(F32(DH)) * jnp.sqrt(tallies.astype(F32)))
    any_spec = pl.BlockSpec(memory_space=pl.ANY)
    smem_spec = pl.BlockSpec(memory_space=pltpu.SMEM)
    rows = seqs * length

    def vmem(*shape):
        return pltpu.VMEM(shape, BF16)

    def dma(*shape):
        return pltpu.SemaphoreType.DMA(shape)

    result = jax.ShapeDtypeStruct(x.shape, BF16)
    row, col = pl.pallas_call(
        functools.partial(kernel, n, seqs, length, width),
        out_shape=(result, result),
        in_specs=[smem_spec, smem_spec] + [any_spec] * 9,
        out_specs=(any_spec, any_spec),
        scratch_shapes=[
            vmem(*x.shape),
            *[vmem(width, width) for _ in range(6)],
            vmem(size, size),
            vmem(size, size),
            vmem(rows, width),
            vmem(rows, width),
            vmem(rows, width),
            vmem(rows, width),
            vmem(groups, (GROUP // DH) * length, length),
            vmem(groups, n // 2, share, length),
            vmem(groups, share, length),
            vmem(groups, share, length),
            vmem(groups, (GROUP // DH) * length, length),
            vmem(*x.shape),
            vmem(steps, size, width),
            vmem(steps, size, width),
            vmem(step_pairs * span, width),
            vmem(step_pairs * span, width),
            vmem(step_pairs * span, width),
            vmem(steps, n, step_rows, width),
            vmem(steps, size, width),
            vmem(*x.shape),
            dma(10 + steps),
            dma(groups, n // 2), dma(groups, n // 2), dma(groups), dma(groups),
            dma(groups, n // 2), dma(groups, n // 2),
            dma(steps, n), dma(steps, n), dma(steps, n), dma(steps, n),
        ],
        compiler_params=pltpu.CompilerParams(
            collective_id=0, has_side_effects=True, vmem_limit_bytes=56 * 1024 * 1024
        ),
    )(tallies, inverse, x, hq, hk, hv, vq, vk, vv, jnp.asarray(there, BF16), jnp.asarray(there.T, BF16))
    return pl.pallas_call(
        hand_on,
        out_shape=(result, result),
        in_specs=[any_spec, any_spec],
        out_specs=(any_spec, any_spec),
        scratch_shapes=[vmem(2, *x.shape), dma(2, seqs), dma(2, seqs)],
    )(row, col)


def solution(mesh):
    in_specs = (P(("aln", "seq"), None, None), P("aln"), P(), P(), P(), P(), P(), P())
    out_specs = (P(("aln", "seq"), None, None), P(("aln", "seq"), None, None))
    return jax.shard_map(local, mesh=mesh, in_specs=in_specs, out_specs=out_specs, check_vma=False)
```

time: 105 us -> 99.9 us (0.951)
  local copies, waits for them, and re-layouts: 3.92 us -> 0 us
    unnamed x4 -> x0, local copies, waits for them, and re-layouts: 3.92 us -> none
    pallas_call x1, Pallas kernels: 99.1 us -> 95.2 us  [local(): pl.pallas_call(functools.partial(kernel, n, seqs, length, width), out_sha...]
    pallas_call x0 -> x1, Pallas kernels: none -> 3.18 us  [local(): pl.pallas_call(hand_on, out_shape=(result, result), in_specs=[any_spec, a...]
where the time goes in v2:
time: 99.9 us; the launch traced here: 99.8 us
  Pallas kernels  98.4 us (98%)
  between operations  1.37 us (1%)
    pallas_call x1, Pallas kernels, local(): pl.pallas_call(functools.partial(kernel, n, seqs, length, width), out_sha...  95.2 us
    pallas_call x1, Pallas kernels, local(): pl.pallas_call(hand_on, out_shape=(result, result), in_specs=[any_spec, a...  3.18 us

profile of v2, /device:TPU:0, one launch (start us, length us, event | category | flops | bytes accessed | tf_op | source)
XLA Modules:
  0.0 99.8 jit_solution(10511068454124521099)
XLA Ops:
  1.4 95.2 %shard_map.113 = (bf16[8,128,768]{2,1,0:T(8,128)(2,1)}, bf16[8,128,768]{2,1,0:T(8,128)(2,1)}) custom-call(s32[1]{0:T(128)S(6)} %copy.12.count_ref, f32[1]{0:T(128)S(6)} %div.3.inv_ref, bf16[8,128,768]{2,1,0:T(8,128)(2,1)} %x_hbm.1, bf16[768,768]{1,0:T(8,128)(2,1)} %hq_hbm.1, bf16[768,768]{1,0:T(8,128)(2,1)} %hk_hbm.1, bf16[768,768]{1,0:T(8,128)(2,1)} %hv_hbm.1, ...), custom_call_target="tpu_custom_call" | custom-call | tf_op jit(solution)/shard_map/pallas_call | solution.py:388
  96.6 3.2 %shard_map.114 = (bf16[8,128,768]{2,1,0:T(8,128)(2,1)}, bf16[8,128,768]{2,1,0:T(8,128)(2,1)}) custom-call(bf16[8,128,768]{2,1,0:T(8,128)(2,1)} %get-tuple-element.4.refs_0_, bf16[8,128,768]{2,1,0:T(8,128)(2,1)} %get-tuple-element.5.refs_1_), custom_call_target="tpu_custom_call" | custom-call | tf_op jit(solution)/shard_map/pallas_call | solution.py:425

commit v3 on v2

--- a/solution.py
+++ b/solution.py
@@ -70,7 +70,7 @@
              (vq_hbm, vq), (vk_hbm, vk), (vv_hbm, vv), (back_hbm, back)]
         )
     ]
-    for load in loads:
+    for load in loads[:3]:
         load.start()
 
     barrier = pltpu.get_barrier_semaphore()
@@ -154,9 +154,11 @@
         normed[aligned(s, length)] = standardize(x[s].astype(F32)).astype(BF16)
         return c
 
-    lax.fori_loop(0, seqs, norm_one, 0)
+    lax.fori_loop(0, seqs, norm_one, 0, unroll=2)
     loads[1].wait()
     loads[2].wait()
+    for load in loads[3:]:
+        load.start()
 
     def beside(ref, lanes):
         return jnp.concatenate(
@@ -185,7 +187,7 @@
             rk[at, lanes] = dot(a, hk[:, lanes]).astype(BF16)
             return c
 
-        lax.fori_loop(0, rows // tile, project, 0)
+        lax.fori_loop(0, rows // tile, project, 0, unroll=True)
         for p in range(GROUP // PAIR):
             two = slice(g * GROUP + p * PAIR, g * GROUP + (p + 1) * PAIR)
             q = beside(rq, two)
@@ -215,12 +217,12 @@
         if g > 0:
             exchange(g - 1)
     loads[3].wait()
-    lax.fori_loop(0, rows // tile // 2, project_v, 0)
+    lax.fori_loop(0, rows // tile // 2, project_v, 0, unroll=True)
     exchange(groups - 1)
-    weigh(0)
-    lax.fori_loop(rows // tile // 2, rows // tile, project_v, 0)
-    for g in range(1, groups):
+    for g in range(groups - 1):
         weigh(g)
+    lax.fori_loop(rows // tile // 2, rows // tile, project_v, 0, unroll=True)
+    weigh(groups - 1)
 
     for g in range(groups):
         near(lambda j: ag_copy(g, j, source(half + j)).wait_recv())

time: 99.9 us -> 98.1 us (0.982)
  Pallas kernels: 98.4 us -> 96.5 us
    pallas_call x1, Pallas kernels: 95.2 us -> 93.4 us  [local(): pl.pallas_call(functools.partial(kernel, n, seqs, length, width), out_sha...]
where the time goes in v3:
time: 98.1 us; the launch traced here: 97.9 us
  Pallas kernels  96.5 us (98%)
  between operations  1.37 us (1%)
    pallas_call x1, Pallas kernels, local(): pl.pallas_call(functools.partial(kernel, n, seqs, length, width), out_sha...  93.4 us
    pallas_call x1, Pallas kernels, local(): pl.pallas_call(hand_on, out_shape=(result, result), in_specs=[any_spec, a...  3.18 us

profile of v3, /device:TPU:0, one launch (start us, length us, event | category | flops | bytes accessed | tf_op | source)
XLA Modules:
  0.0 97.9 jit_solution(826032330391881975)
XLA Ops:
  1.4 93.4 %shard_map.113 = (bf16[8,128,768]{2,1,0:T(8,128)(2,1)}, bf16[8,128,768]{2,1,0:T(8,128)(2,1)}) custom-call(s32[1]{0:T(128)S(6)} %copy.12.count_ref, f32[1]{0:T(128)S(6)} %div.3.inv_ref, bf16[8,128,768]{2,1,0:T(8,128)(2,1)} %x_hbm.1, bf16[768,768]{1,0:T(8,128)(2,1)} %hq_hbm.1, bf16[768,768]{1,0:T(8,128)(2,1)} %hk_hbm.1, bf16[768,768]{1,0:T(8,128)(2,1)} %hv_hbm.1, ...), custom_call_target="tpu_custom_call" | custom-call | tf_op jit(solution)/shard_map/pallas_call | solution.py:390
  94.7 3.2 %shard_map.114 = (bf16[8,128,768]{2,1,0:T(8,128)(2,1)}, bf16[8,128,768]{2,1,0:T(8,128)(2,1)}) custom-call(bf16[8,128,768]{2,1,0:T(8,128)(2,1)} %get-tuple-element.4.refs_0_, bf16[8,128,768]{2,1,0:T(8,128)(2,1)} %get-tuple-element.5.refs_1_), custom_call_target="tpu_custom_call" | custom-call | tf_op jit(solution)/shard_map/pallas_call | solution.py:427
